TPU v7x, 32 devices: a whole 2x2x4 slice. The times are simulated.
32 devices in a mesh: vox: 4 (over y, core), filt: 8 (over z, x).
Axes of the slice: x: 2, y: 2, z: 4, core: 2. Of those that a mesh axis runs over, the one named last changes fastest.
Arguments:
- volume: bfloat16 [1024, 16, 128], P('filt', 'vox'), may hold values from -6 to 6
- kernel: bfloat16 [27, 1024, 1024], P(None, 'filt', 'vox'), may hold values from -0.0390625 to 0.0390625
- bias: float32 [1024], P('filt'), may hold values from -3 to 3
Outputs:
- features: bfloat16 [1024, 16, 128], P('filt', 'vox')
All inputs are finite; a program needn't handle non-finite values.
Results may differ from a plain program's by a relative error of at most 0.001.
Values may be sent and summed in bfloat16 or wider, within the bound.
A program may use at most 64 MiB of HBM per device.

v0:
```python
import jax
import jax.numpy as jnp
from jax import lax
from jax.sharding import PartitionSpec as P

H = 4
W = 32


def padded(block, sides, width):
    for axis, dim in sides:
        count = lax.axis_size(axis)
        forward = [(i, i + 1) for i in range(count - 1)]
        backward = [(target, source) for source, target in forward]
        low = lax.ppermute(
            lax.slice_in_dim(block, block.shape[dim] - width, None, axis=dim), axis, forward
        )
        high = lax.ppermute(lax.slice_in_dim(block, 0, width, axis=dim), axis, backward)
        block = jnp.concatenate([low, block, high], axis=dim)
    return block


def convolve(planes, weights):
    channels = planes.shape[0]
    stack = planes.shape[1]
    filters = weights.shape[3]
    shaped = planes.reshape(1, channels, stack, H, W)
    summed = lax.conv_general_dilated(
        shaped,
        weights,
        (1, 1, 1),
        [(0, 0), (1, 1), (1, 1)],
        dimension_numbers=("NCDHW", "DHWOI", "NCDHW"),
        preferred_element_type=jnp.float32,
    )
    return summed[0].reshape(filters, stack - 2, H * W)


def shards(volume, kernel, bias):
    gathered = lax.all_gather(kernel, "vox", axis=2, tiled=True)
    filters = gathered.shape[1]
    kernel_taps = gathered.reshape(3, 3, 3, filters, gathered.shape[2])
    whole = lax.all_gather(volume, "filt", axis=0, tiled=True)
    rimmed = padded(whole, (("vox", 1),), 1)
    summed = convolve(rimmed, kernel_taps)
    return (summed + bias[:, None, None]).astype(jnp.bfloat16)


def solution(mesh):
    in_specs = (P("filt", "vox", None), P(None, "filt", "vox"), P("filt"))
    out_specs = P("filt", "vox", None)
    return jax.shard_map(shards, mesh=mesh, in_specs=in_specs, out_specs=out_specs, check_vma=False)
```

profile of v0, /device:TPU:0, one launch (start us, length us, event | category | flops | bytes accessed | tf_op | source)
XLA Modules:
  0.0 124.2 jit_solution(1016782855541893228)
XLA Ops:
  6.5 0.0 all-gather.3.cloned.1.call-start
  6.5 1.7 %copy.4 = bf16[128,4,128]{0,2,1:T(8,128)(2,1)} copy(bf16[128,4,128]{2,1,0:T(4,128)(2,1)} %param.3) | data formatting | bytes 262144 | tf_op args[0]
  8.2 0.0 all-gather.3.cloned.1.call-update
  8.2 0.0 all-gather.5.cloned.1.call-start
  8.3 0.7 all-gather.5.cloned.1.call-update
  9.0 42.7 %all-gather.3.cloned.1.call-done = bf16[1024,4,128]{0,2,1:T(8,128)(2,1)} async-done(((bf16[128,4,128]{0,2,1:T(8,128)(2,1)}), bf16[1024,4,128]{0,2,1:T(8,128)(2,1)}) %all-gather.3.cloned.1.call-update) | async-done | bytes 1048592 | tf_op jit(solution)/shard_map/all_gather | solution.py:43
  51.7 1.1 fusion.15
  52.7 1.3 %collective-permute-start = (bf16[1024,1,128]{0,2,1:T(8,128)(2,1)S(1)}, bf16[1024,1,128]{0,2,1:T(8,128)(2,1)S(1)}, u32[]{:S(2)}, u32[]{:S(2)}) collective-permute-start(bf16[1024,1,128]{0,2,1:T(8,128)(2,1)S(1)} %get-tuple-element.5), channel_id=1, source_target_pairs={{0,8},{8,16},{16,24},{1,9},{9,17},{17,25},{2,10},{10,18},{18,26},{... | collective-permute-start | bytes 786440 | tf_op jit(solution)/shard_map/ppermute | solution.py:15
  54.0 1.3 %collective-permute-start.1 = (bf16[1024,1,128]{0,2,1:T(8,128)(2,1)S(1)}, bf16[1024,1,128]{0,2,1:T(8,128)(2,1)S(1)}, u32[]{:S(2)}, u32[]{:S(2)}) collective-permute-start(bf16[1024,1,128]{0,2,1:T(8,128)(2,1)S(1)} %get-tuple-element.6), channel_id=1, source_target_pairs={{8,0},{16,8},{24,16},{9,1},{17,9},{25,17},{10,2},{18,10},{26,18},{... | collective-permute-start | bytes 786440 | tf_op jit(solution)/shard_map/ppermute | solution.py:18
  55.3 0.0 collective-permute-done
  55.4 3.9 %collective-permute-done.1 = bf16[1024,1,128]{0,2,1:T(8,128)(2,1)S(1)} collective-permute-done((bf16[1024,1,128]{0,2,1:T(8,128)(2,1)S(1)}, bf16[1024,1,128]{0,2,1:T(8,128)(2,1)S(1)}, u32[]{:S(2)}, u32[]{:S(2)}) %collective-permute-start.1) | collective-permute-done | bytes 262176 | tf_op jit(solution)/shard_map/ppermute | solution.py:18
  59.2 1.6 %pad_maximum_fusion = bf16[1024,6,128]{0,2,1:T(8,128)(2,1)S(1)} fusion(bf16[1024,1,128]{0,2,1:T(8,128)(2,1)S(1)} %collective-permute-done.1, bf16[1024,4,128]{0,2,1:T(8,128)(2,1)} %all-gather.3.cloned.1.call-done, bf16[1024,1,128]{0,2,1:T(8,128)(2,1)S(1)} %collective-permute-done), kind=kLoop, calls=%fused_computation.8 | loop fusion | flops 1572864 | bytes 3145728 | tf_op jit(solution)/shard_map/concatenate | solution.py:19
  60.8 1.2 copy.11
  62.0 0.8 pad.clone
  62.9 0.0 copy-start.1
  62.9 0.6 copy.7
  63.5 0.2 slice.12
  63.7 41.0 %all-gather.5.cloned.1.call-done = bf16[27,128,1024]{2,1,0:T(8,128)(2,1)} async-done(((bf16[27,128,256]{2,1,0:T(8,128)(2,1)}), bf16[27,128,1024]{2,1,0:T(8,128)(2,1)}) %all-gather.5.cloned.1.call-update) | async-done | bytes 7077904 | tf_op jit(solution)/shard_map/all_gather | solution.py:40
  104.8 0.0 copy-done.1
  104.8 0.0 copy-start
  104.8 11.6 %fusion.9 = f32[4,4,8,5,128]{4,2,3,1,0:T(8,128)S(1)} fusion(bf16[3,3,3,128,1024]{4,3,2,1,0:T(8,128)(2,1)} %bitcast.17, bf16[1024,6,4,1,7,2]{0,4,5,2,1,3:T(8,128)(2,1)S(1)} %slice.12, bf16[1024,6,4,1,8,5]{0,4,5,2,1,3:T(8,128)(2,1)S(1)} %copy.7, pred[8,5]{0,1:T(8,128)(4,1)S(1)} %copy-done.1), kind=kOutput, calls=%fused_computation.10 | convolution fusion | flops 3783213056 | bytes 10059816 | tf_op jit(solution)/shard_map/conv_general_dilated | solution.py:28
  116.3 0.1 copy.8
  116.5 0.0 copy-done
  116.5 0.8 copy.10
  (3 shorter events, 0.1 us)
Async XLA Ops:
  6.5 45.1 %all-gather.3.cloned.1.call-start = ((), (), s32[]{:S(2)}) async-start(), calls=%async_computation | async-start | bytes 1179648 | tf_op jit(solution)/shard_map/all_gather | solution.py:43
  8.2 96.5 %all-gather.5.cloned.1.call-start = ((), (), s32[]{:S(2)}) async-start(), calls=%async_computation.1 | async-start | bytes 8847360 | tf_op jit(solution)/shard_map/all_gather | solution.py:40
  52.7 2.6 %collective-permute-start = (bf16[1024,1,128]{0,2,1:T(8,128)(2,1)S(1)}, bf16[1024,1,128]{0,2,1:T(8,128)(2,1)S(1)}, u32[]{:S(2)}, u32[]{:S(2)}) collective-permute-start(bf16[1024,1,128]{0,2,1:T(8,128)(2,1)S(1)} %get-tuple-element.5), channel_id=1, source_target_pairs={{0,8},{8,16},{16,24},{1,9},{9,17},{17,25},{2,10},{10,18},{18,26},{... | collective-permute-start | bytes 786440 | tf_op jit(solution)/shard_map/ppermute | solution.py:15
  54.0 5.2 %collective-permute-start.1 = (bf16[1024,1,128]{0,2,1:T(8,128)(2,1)S(1)}, bf16[1024,1,128]{0,2,1:T(8,128)(2,1)S(1)}, u32[]{:S(2)}, u32[]{:S(2)}) collective-permute-start(bf16[1024,1,128]{0,2,1:T(8,128)(2,1)S(1)} %get-tuple-element.6), channel_id=1, source_target_pairs={{8,0},{16,8},{24,16},{9,1},{17,9},{25,17},{10,2},{18,10},{26,18},{... | collective-permute-start | bytes 786440 | tf_op jit(solution)/shard_map/ppermute | solution.py:18
  62.9 41.9 %copy-start.1 = (pred[8,5]{0,1:T(8,128)(4,1)S(1)}, pred[8,5]{0,1:T(8,128)(4,1)}, u32[]{:S(2)}) copy-start(pred[8,5]{0,1:T(8,128)(4,1)} %constant.4) | copy-start | bytes 124
  104.8 11.7 %copy-start = (f32[128]{0:T(128)S(1)}, f32[128]{0:T(128)}, u32[]{:S(2)}) copy-start(f32[128]{0:T(128)} %param.5) | copy-start | bytes 1540
Sparse Core Ops, SparseCore 0:
  9.4 42.2 all-gather.2
  53.2 51.5 all-gather.4
where the time goes:
time: 124 us
  waiting for transfers between devices  88.3 us (71%)
  between operations  13.5 us (11%)
  matrix products  11.6 us (9%)
  local copies, waits for them, and re-layouts  6.55 us (5%)
  starting transfers between devices  2.64 us (2%)
  other arithmetic  1.58 us (1%)
    all_gather x1, waiting for transfers between devices, shards(): whole = lax.all_gather(volume, 'filt', axis=0, tiled=True)  42.7 us
    all_gather x1, waiting for transfers between devices, shards(): gathered = lax.all_gather(kernel, 'vox', axis=2, tiled=True)  41 us
    conv_general_dilated x1, matrix products, convolve(): lax.conv_general_dilated(shaped, weights, (1, 1, 1), [(0, 0), (1, 1), (1,...  11.6 us
    ppermute x1, waiting for transfers between devices, padded(): lax.ppermute(lax.slice_in_dim(block, 0, width, axis=dim), axis, backward)  3.88 us
    unnamed x6, local copies, waits for them, and re-layouts  2.9 us
  transfers between devices with their start and end apart: 4, of which 3 were waited for; matrix products, arithmetic and copies ran while one was open for 4% of the time, Pallas kernels for 0%

commit v1 on v0

v1 whole, which is shorter than its diff:
```python
import functools

import jax
import jax.numpy as jnp
from jax import lax
from jax.experimental import pallas as pl
from jax.experimental.pallas import tpu as pltpu
from jax.sharding import PartitionSpec as P

H = 4
W = 32
MESH = pl.DeviceIdType.MESH


def body(
    nv, rep, vol, ker, out, held, slab, taps, prod, mine, away, near, far,
    tap_sem, own_sem, s1, r1, s2, r2, s3, r3, s4, r4, s5, r5,
):
    v = lax.axis_index("vox")
    f = lax.axis_index("filt")
    q = lax.div(f, rep)
    s = lax.rem(f, rep)
    planes, chans, cells = vol.shape
    filters = taps.shape[2]
    depth = taps.shape[3]
    half = nv // 2
    pair = lax.div(v, 2)
    core = lax.rem(v, 2)
    sibling = v + 1 - 2 * core

    load = pltpu.make_async_copy(ker, taps, tap_sem)
    load.start()

    barrier = pltpu.get_barrier_semaphore()
    peers = []
    for k in range(1, nv):
        peers.append((v, lax.rem(q + k, nv) * rep + s))
        peers.append((lax.rem(v + k, nv), f))
    for t in range(1, rep):
        peers.append((v, q * rep + lax.rem(s + t, rep)))
    for peer in peers:
        pl.semaphore_signal(barrier, inc=1, device_id=peer, device_id_type=MESH)
    pl.semaphore_wait(barrier, len(peers))

    def spot(owner, part):
        rows = pl.ds(pl.multiple_of(part * chans, chans), chans)
        return slab.at[pl.ds(1 + owner * planes, planes), rows, :]

    def gather_copy(k):
        return pltpu.make_async_remote_copy(
            vol, held.at[k], s1.at[k], r1.at[k],
            device_id=(v, lax.rem(q + k, nv) * rep + s), device_id_type=MESH)

    def cross_copy(src, k, target):
        return pltpu.make_async_remote_copy(
            src, spot(v, s), s2.at[k], r2.at[lax.rem(v - target + nv, nv)],
            device_id=(target, f), device_id_type=MESH)

    def side_copy(src, owner, j, t):
        return pltpu.make_async_remote_copy(
            src, spot(owner, s), s3.at[t, j], r3.at[t, j],
            device_id=(v, q * rep + lax.rem(s + t, rep)), device_id_type=MESH)

    def pass_on(k):
        origin = lax.rem(q - k + nv, nv)
        src = vol if k == 0 else held.at[k]

        @pl.when(origin == v)
        def _():
            for t in range(1, rep):
                side_copy(src, v, 0, t).start()
            pltpu.make_async_copy(src, spot(v, s), own_sem).start()

        @pl.when(origin != v)
        def _():
            cross_copy(src, k, origin).start()

    for k in range(1, nv):
        gather_copy(k).start()
    pass_on(0)
    zero = jnp.zeros((1,) + slab.shape[1:], slab.dtype)
    slab[pl.ds(0, 1)] = zero
    slab[pl.ds(slab.shape[0] - 1, 1)] = zero
    for k in range(1, nv):
        gather_copy(k).wait_recv()
        pass_on(k)
    for j in range(1, nv):
        owner = lax.rem(v + j, nv)
        pltpu.make_async_remote_copy(
            vol, spot(owner, s), s2.at[0], r2.at[j],
            device_id=(owner, f), device_id_type=MESH).wait_recv()
        for t in range(1, rep):
            side_copy(spot(owner, s), owner, j, t).start()
    pltpu.make_async_copy(vol, spot(v, s), own_sem).wait()
    load.wait()
    for j in range(nv):
        owner = lax.rem(v + j, nv)
        for t in range(1, rep):
            part = lax.rem(s - t + rep, rep)
            pltpu.make_async_remote_copy(
                vol, spot(owner, part), s3.at[t, j], r3.at[t, j],
                device_id=(v, q * rep + part), device_id_type=MESH).wait_recv()

    lane = lax.broadcasted_iota(jnp.int32, (filters, cells), 1)
    row = lane // W
    col = lane % W

    def shifted(x, step, keep):
        return jnp.where(keep, pltpu.roll(x, (-step) % cells, 1), 0.0)

    def convolve(block, dest):
        def step(i, carry):
            base = block * planes + 2 * i
            xs = [slab[base + a] for a in range(4)]
            cols = [jnp.concatenate([xs[a], xs[a + 1]], axis=1) for a in range(3)]
            if depth % 128 == 0:
                rhs = jnp.concatenate(cols, axis=0)
                for b in range(3):
                    lhs = jnp.concatenate(
                        [taps[a, pl.ds(3 * b, 3)].reshape(3 * filters, depth) for a in range(3)], axis=1)
                    prod[pl.ds(3 * b * filters, 3 * filters)] = jnp.dot(
                        lhs, rhs, preferred_element_type=jnp.float32)
            else:
                for b in range(3):
                    prod[pl.ds(3 * b * filters, 3 * filters)] = sum(
                        jnp.dot(taps[a, pl.ds(3 * b, 3)].reshape(3 * filters, depth), cols[a],
                                preferred_element_type=jnp.float32) for a in range(3))
            for side in range(2):
                total = None
                for b in range(3):
                    part = None
                    for e in range(3):
                        x = prod[pl.ds((3 * b + e) * filters, filters), pl.ds(side * cells, cells)]
                        if e != 1:
                            x = shifted(x, e - 1, (col + e >= 1) & (col + e <= W))
                        part = x if part is None else part + x
                    if b != 1:
                        part = shifted(part, (b - 1) * W, (row + b >= 1) & (row + b <= H))
                    total = part if total is None else total + part
                dest[2 * i + side] = total
            return carry
        lax.fori_loop(0, planes // 2, step, 0)

    def near_copy(m):
        return pltpu.make_async_remote_copy(
            away.at[m], near.at[m], s4.at[m], r4.at[m],
            device_id=(sibling, f), device_id_type=MESH)

    def far_copy(m):
        return pltpu.make_async_remote_copy(
            mine.at[m], far.at[m], s5.at[m], r5.at[m],
            device_id=(2 * lax.rem(pair + m, half) + core, f), device_id_type=MESH)

    for m in list(range(1, half)) + [0]:
        other = 2 * lax.rem(pair + m, half)
        convolve(other + 1 - core, away.at[m])
        near_copy(m).start()
        convolve(other + core, mine.at[m])
        near_copy(m).wait_recv()
        if m > 0:
            mine[m] = mine[m] + near[m]
            far_copy(m).start()
    total = mine[0] + near[0]
    for m in range(1, half):
        far_copy(m).wait_recv()
        total = total + far[m]
    out[...] = total

    for k in range(1, nv):
        gather_copy(k).wait_send()
    for k in range(nv):
        origin = lax.rem(q - k + nv, nv)

        @pl.when(origin != v)
        def _():
            cross_copy(vol, k, origin).wait_send()
    for j in range(nv):
        for t in range(1, rep):
            side_copy(vol, v, j, t).wait_send()
    for m in range(half):
        near_copy(m).wait_send()
        if m > 0:
            far_copy(m).wait_send()


def shards(nv, nf, volume, kernel, bias):
    rep = nf // nv
    chans, planes, cells = volume.shape
    filters, depth = kernel.shape[1:]
    half = nv // 2
    blocks = jnp.transpose(volume, (1, 0, 2))
    taps = kernel.reshape(3, 9, filters, depth)
    part = (half, planes, filters, cells)
    dma = pltpu.SemaphoreType.DMA
    total = pl.pallas_call(
        functools.partial(body, nv, rep),
        out_shape=jax.ShapeDtypeStruct((planes, filters, cells), jnp.float32),
        in_specs=[pl.BlockSpec(memory_space=pltpu.VMEM), pl.BlockSpec(memory_space=pl.ANY)],
        out_specs=pl.BlockSpec(memory_space=pltpu.VMEM),
        scratch_shapes=[
            pltpu.VMEM((nv, planes, chans, cells), jnp.bfloat16),
            pltpu.VMEM((nv * planes + 2, depth, cells), jnp.bfloat16),
            pltpu.VMEM((3, 9, filters, depth), jnp.bfloat16),
            pltpu.VMEM((9 * filters, 2 * cells), jnp.float32),
            pltpu.VMEM(part, jnp.float32),
            pltpu.VMEM(part, jnp.float32),
            pltpu.VMEM(part, jnp.float32),
            pltpu.VMEM(part, jnp.float32),
            dma, dma, dma((nv,)), dma((nv,)), dma((nv,)), dma((nv,)),
            dma((rep, nv)), dma((rep, nv)), dma((half,)), dma((half,)), dma((half,)), dma((half,)),
        ],
        compiler_params=pltpu.CompilerParams(
            collective_id=0, has_side_effects=True, vmem_limit_bytes=40 * 1024 * 1024),
        cost_estimate=pl.CostEstimate(
            flops=2 * 27 * filters * depth * nv * planes * cells,
            bytes_accessed=2 * 27 * filters * depth, transcendentals=0),
    )(blocks, taps)
    summed = jnp.transpose(total, (1, 0, 2)) + bias[:, None, None]
    return summed.astype(jnp.bfloat16)


def solution(mesh):
    in_specs = (P("filt", "vox", None), P(None, "filt", "vox"), P("filt"))
    out_specs = P("filt", "vox", None)
    work = functools.partial(shards, mesh.shape["vox"], mesh.shape["filt"])
    return jax.shard_map(work, mesh=mesh, in_specs=in_specs, out_specs=out_specs, check_vma=False)
```

time: 124 us -> 43.7 us (0.35)
  the two profiles are of different devices: /device:TPU:0 before, /device:TPU:28 now
where the time goes in v1:
time: 43.7 us; the launch traced here: 43.5 us
  Pallas kernels  40.3 us (92%)
  local copies, waits for them, and re-layouts  3.16 us (7%)
    pallas_call x1, Pallas kernels, shards(): pl.pallas_call(functools.partial(body, nv, rep), out_shape=jax.ShapeDtype...  40.3 us
    unnamed x5, local copies, waits for them, and re-layouts  2.4 us

profile of v1, /device:TPU:28, one launch (start us, length us, event | category | flops | bytes accessed | tf_op | source)
XLA Modules:
  0.0 43.5 jit_solution(13983971616633537983)
XLA Ops:
  0.0 0.9 %copy.7 = bf16[128,4,128]{2,0,1:T(8,128)(2,1)S(1)} copy(bf16[128,4,128]{2,1,0:T(4,128)(2,1)} %param.3) | data formatting | bytes 262144 | tf_op args[0]
  0.9 0.0 copy-start
  0.9 1.5 %copy-done = bf16[27,128,256]{2,1,0:T(8,128)(2,1)S(1)} copy-done((bf16[27,128,256]{2,1,0:T(8,128)(2,1)S(1)}, bf16[27,128,256]{2,1,0:T(8,128)(2,1)}, u32[]{:S(2)}) %copy-start) | copy-done | bytes 1769496
  2.4 0.0 copy-start.1
  2.4 40.3 %shard_map.37 = f32[4,128,128]{2,1,0:T(8,128)S(1)} custom-call(bf16[4,128,128]{2,1,0:T(8,128)(2,1)S(1)} %bitcast.6, bf16[3,9,128,256]{3,2,1,0:T(8,128)(2,1)S(1)} %bitcast.7), custom_call_target="tpu_custom_call" | custom-call | flops 3623878656 | bytes 1769472 | tf_op jit(solution)/shard_map/pallas_call | solution.py:195
  42.7 0.0 copy-done.1
  42.7 0.1 fusion
  42.8 0.8 %copy.5 = bf16[128,4,128]{2,1,0:T(4,128)(2,1)} copy(bf16[128,4,128]{2,0,1:T(8,128)(2,1)S(1)} %fusion) | data formatting | bytes 262144 | tf_op jit(solution)/shard_map/convert_element_type | solution.py:219
Async XLA Ops:
  0.9 1.5 %copy-start = (bf16[27,128,256]{2,1,0:T(8,128)(2,1)S(1)}, bf16[27,128,256]{2,1,0:T(8,128)(2,1)}, u32[]{:S(2)}) copy-start(bf16[27,128,256]{2,1,0:T(8,128)(2,1)} %param.4) | copy-start | bytes 5308420
  2.4 40.3 %copy-start.1 = (f32[128]{0:T(128)S(1)}, f32[128]{0:T(128)}, u32[]{:S(2)}) copy-start(f32[128]{0:T(128)} %param.5) | copy-start | bytes 1540

commit v2 on v1

v2 whole, which is shorter than its diff:
```python
import functools

import jax
import jax.numpy as jnp
from jax import lax
from jax.experimental import pallas as pl
from jax.experimental.pallas import tpu as pltpu
from jax.sharding import PartitionSpec as P

H = 4
W = 32
CHUNKS = 2
MESH = pl.DeviceIdType.MESH


def body(
    nv, rep, vol, ker, out, held, slab, taps, prod, mine, away, near, far,
    tap_sem, own_sem, s1, r1, s2, r2, s3, r3, s4, r4, s5, r5,
):
    v = lax.axis_index("vox")
    f = lax.axis_index("filt")
    q = lax.div(f, rep)
    s = lax.rem(f, rep)
    planes, chans, cells = vol.shape
    filters = taps.shape[2]
    depth = taps.shape[3]
    half = nv // 2
    pair = lax.div(v, 2)
    core = lax.rem(v, 2)
    sibling = v + 1 - 2 * core

    load = pltpu.make_async_copy(ker, taps, tap_sem)
    load.start()

    def vox_at(dp, dc):
        return 2 * lax.rem(pair + dp, half) + lax.rem(core + dc, 2)

    offsets = [(dp, dc) for dp in range(half) for dc in range(2)]
    barrier = pltpu.get_barrier_semaphore()
    peers = [(v, lax.rem(q + k, nv) * rep + s) for k in (1, nv - 1)]
    peers += [(vox_at(dp, dc), f) for dp, dc in offsets[1:]]
    peers += [(v, q * rep + lax.rem(s + t, rep)) for t in range(1, rep)]
    for peer in peers:
        pl.semaphore_signal(barrier, inc=1, device_id=peer, device_id_type=MESH)
    pl.semaphore_wait(barrier, len(peers))

    size = planes // CHUNKS

    def spot(owner, part, piece):
        rows = pl.ds(pl.multiple_of(part * chans, chans), chans)
        return slab.at[pl.ds(1 + owner * planes + piece * size, size), rows, :]

    def own(piece):
        return vol.at[pl.ds(piece * size, size)]

    def hold(origin, piece):
        return held.at[origin, pl.ds(piece * size, size)]

    def line_copy(src, origin, piece, way):
        target = q + 1 if way == 0 else q - 1
        return pltpu.make_async_remote_copy(
            src, hold(origin, piece), s1.at[way, origin, piece], r1.at[origin, piece],
            device_id=(v, target * rep + s), device_id_type=MESH)

    def cross_copy(src, target, piece):
        place = 2 * lax.rem(pair - lax.div(target, 2) + half, half) + lax.rem(core + target, 2)
        return pltpu.make_async_remote_copy(
            src, spot(v, s, piece), s2.at[target, piece], r2.at[place, piece],
            device_id=(target, f), device_id_type=MESH)

    def side_copy(src, owner, place, piece, t):
        return pltpu.make_async_remote_copy(
            src, spot(owner, s, piece), s3.at[t, place, piece], r3.at[t, place, piece],
            device_id=(v, q * rep + lax.rem(s + t, rep)), device_id_type=MESH)

    first_dc = lax.rem(1 + pair + core, 2)
    owner_first = first_dc == 0

    def spread(src, origin, piece):
        @pl.when(origin == v)
        def _():
            @pl.when(owner_first)
            def _():
                for t in range(1, rep):
                    side_copy(src, v, 0, piece, t).start()
            pltpu.make_async_copy(src, spot(v, s, piece), own_sem.at[piece]).start()

        @pl.when(origin != v)
        def _():
            cross_copy(src, origin, piece).start()

    def own_wait(piece):
        pltpu.make_async_copy(own(piece), spot(v, s, piece), own_sem.at[piece]).wait()

    def pass_side(dp, dc, piece):
        place = 2 * dp + dc
        owner = vox_at(dp, dc)
        if place == 0:
            own_wait(piece)
        else:
            pltpu.make_async_remote_copy(
                own(piece), spot(owner, s, piece), s2.at[0, piece], r2.at[place, piece],
                device_id=(owner, f), device_id_type=MESH).wait_recv()
        for t in range(1, rep):
            side_copy(spot(owner, s, piece), owner, place, piece, t).start()

    def relay(piece):
        @pl.when(jnp.logical_not(owner_first))
        def _():
            pass_side(0, 1, piece)
        for dp, dc in offsets[2:]:
            pass_side(dp, dc, piece)

        if piece == CHUNKS - 1:
            for late in range(CHUNKS):
                @pl.when(owner_first)
                def _():
                    pass_side(0, 1, late)

                @pl.when(jnp.logical_not(owner_first))
                def _():
                    pass_side(0, 0, late)

    far_off = jnp.abs(v - q)
    for piece in range(CHUNKS):
        @pl.when(q < nv - 1)
        def _():
            line_copy(own(piece), q, piece, 0).start()

        @pl.when(q > 0)
        def _():
            line_copy(own(piece), q, piece, 1).start()

    for piece in range(CHUNKS):
        spread(own(piece), q, piece)
    zero = jnp.zeros((1,) + slab.shape[1:], slab.dtype)
    slab[pl.ds(0, 1)] = zero
    slab[pl.ds(slab.shape[0] - 1, 1)] = zero
    waiting = [(0, piece) for piece in range(CHUNKS)]
    for d in range(1, nv):
        for piece in range(CHUNKS):
            @pl.when(q >= d)
            def _():
                origin = q - d
                line_copy(own(piece), origin, piece, 0).wait_recv()

                @pl.when(q < nv - 1)
                def _():
                    line_copy(hold(origin, piece), origin, piece, 0).start()
                spread(hold(origin, piece), origin, piece)

            @pl.when(q + d < nv)
            def _():
                origin = q + d
                line_copy(own(piece), origin, piece, 1).wait_recv()

                @pl.when(q > 0)
                def _():
                    line_copy(hold(origin, piece), origin, piece, 1).start()
                spread(hold(origin, piece), origin, piece)

            waiting.append((d, piece))
            if len(waiting) > CHUNKS:
                first, late = waiting.pop(0)

                @pl.when(far_off == first)
                def _():
                    relay(late)

    for first, late in waiting:
        @pl.when(far_off == first)
        def _():
            relay(late)

    @pl.when(owner_first)
    def _():
        for piece in range(CHUNKS):
            own_wait(piece)
    load.wait()

    def arrived(dp, dc):
        owner = vox_at(dp, dc)
        place = 2 * dp + dc
        for piece in range(CHUNKS):
            for t in range(1, rep):
                part = lax.rem(s - t + rep, rep)
                pltpu.make_async_remote_copy(
                    own(piece), spot(owner, part, piece), s3.at[t, place, piece], r3.at[t, place, piece],
                    device_id=(v, q * rep + part), device_id_type=MESH).wait_recv()

    arrived(0, first_dc)
    for dp, dc in offsets[2:]:
        arrived(dp, dc)
    if half != 2:
        arrived(0, 1 - first_dc)

    lane = lax.broadcasted_iota(jnp.int32, (filters, cells), 1)
    row = lane // W
    col = lane % W

    def shifted(x, step, keep):
        return jnp.where(keep, pltpu.roll(x, (-step) % cells, 1), 0.0)

    def convolve(block, dest, i):
        base = block * planes + 2 * i
        xs = [slab[base + a] for a in range(4)]
        cols = [jnp.concatenate([xs[a], xs[a + 1]], axis=1) for a in range(3)]
        if depth % 128 == 0:
            rhs = jnp.concatenate(cols, axis=0)
            for b in range(3):
                lhs = jnp.concatenate(
                    [taps[a, pl.ds(3 * b, 3)].reshape(3 * filters, depth) for a in range(3)], axis=1)
                prod[pl.ds(3 * b * filters, 3 * filters)] = jnp.dot(
                    lhs, rhs, preferred_element_type=jnp.float32)
        else:
            for b in range(3):
                prod[pl.ds(3 * b * filters, 3 * filters)] = sum(
                    jnp.dot(taps[a, pl.ds(3 * b, 3)].reshape(3 * filters, depth), cols[a],
                            preferred_element_type=jnp.float32) for a in range(3))
        for side in range(2):
            total = None
            for b in range(3):
                part = None
                for e in range(3):
                    x = prod[pl.ds((3 * b + e) * filters, filters), pl.ds(side * cells, cells)]
                    if e != 1:
                        x = shifted(x, e - 1, (col + e >= 1) & (col + e <= W))
                    part = x if part is None else part + x
                if b != 1:
                    part = shifted(part, (b - 1) * W, (row + b >= 1) & (row + b <= H))
                total = part if total is None else total + part
            dest[2 * i + side] = total

    def near_copy(m, i):
        return pltpu.make_async_remote_copy(
            away.at[m, pl.ds(2 * i, 2)], near.at[m, pl.ds(2 * i, 2)], s4.at[m, i], r4.at[m, i],
            device_id=(sibling, f), device_id_type=MESH)

    def far_copy(m, i):
        return pltpu.make_async_remote_copy(
            mine.at[m, pl.ds(2 * i, 2)], far.at[m, pl.ds(2 * i, 2)], s5.at[m, i], r5.at[m, i],
            device_id=(2 * lax.rem(pair + m, half) + core, f), device_id_type=MESH)

    steps = planes // 2
    for m in list(range(1, half)) + [0]:
        other = 2 * lax.rem(pair + m, half)
        if m == 0 and half == 2:
            arrived(0, 1 - first_dc)

        def work(i, carry):
            rows = pl.ds(2 * i, 2)
            convolve(other + 1 - core, away.at[m], i)
            near_copy(m, i).start()
            convolve(other + core, mine.at[m], i)
            if m > 0:
                near_copy(m, i).wait_recv()
                mine[m, rows] = mine[m, rows] + near[m, rows]
                far_copy(m, i).start()
            return carry
        lax.fori_loop(0, steps, work, 0)
    for i in range(steps):
        rows = pl.ds(2 * i, 2)
        near_copy(0, i).wait_recv()
        total = mine[0, rows] + near[0, rows]
        for m in range(1, half):
            far_copy(m, i).wait_recv()
            total = total + far[m, rows]
        out[rows] = total

    for piece in range(CHUNKS):
        for origin in range(nv):
            @pl.when((origin <= q) & (q < nv - 1))
            def _():
                line_copy(own(piece), origin, piece, 0).wait_send()

            @pl.when((origin >= q) & (q > 0))
            def _():
                line_copy(own(piece), origin, piece, 1).wait_send()

            @pl.when(origin != v)
            def _():
                cross_copy(own(piece), origin, piece).wait_send()
        for place in range(nv):
            for t in range(1, rep):
                side_copy(own(piece), v, place, piece, t).wait_send()
    for m in range(half):
        for i in range(steps):
            near_copy(m, i).wait_send()
            if m > 0:
                far_copy(m, i).wait_send()


def shards(nv, nf, volume, kernel, bias):
    rep = nf // nv
    chans, planes, cells = volume.shape
    filters, depth = kernel.shape[1:]
    half = nv // 2
    steps = planes // 2
    blocks = jnp.transpose(volume, (1, 0, 2))
    taps = kernel.reshape(3, 9, filters, depth)
    part = (half, planes, filters, cells)
    dma = pltpu.SemaphoreType.DMA
    total = pl.pallas_call(
        functools.partial(body, nv, rep),
        out_shape=jax.ShapeDtypeStruct((planes, filters, cells), jnp.float32),
        in_specs=[pl.BlockSpec(memory_space=pltpu.VMEM), pl.BlockSpec(memory_space=pl.ANY)],
        out_specs=pl.BlockSpec(memory_space=pltpu.VMEM),
        scratch_shapes=[
            pltpu.VMEM((nv, planes, chans, cells), jnp.bfloat16),
            pltpu.VMEM((nv * planes + 2, depth, cells), jnp.bfloat16),
            pltpu.VMEM((3, 9, filters, depth), jnp.bfloat16),
            pltpu.VMEM((9 * filters, 2 * cells), jnp.float32),
            pltpu.VMEM(part, jnp.float32),
            pltpu.VMEM(part, jnp.float32),
            pltpu.VMEM(part, jnp.float32),
            pltpu.VMEM(part, jnp.float32),
            dma, dma((CHUNKS,)), dma((2, nv, CHUNKS)), dma((nv, CHUNKS)), dma((nv, CHUNKS)), dma((nv, CHUNKS)),
            dma((rep, nv, CHUNKS)), dma((rep, nv, CHUNKS)), dma((half, steps)), dma((half, steps)), dma((half, steps)), dma((half, steps)),
        ],
        compiler_params=pltpu.CompilerParams(
            collective_id=0, has_side_effects=True, vmem_limit_bytes=60 * 1024 * 1024),
        cost_estimate=pl.CostEstimate(
            flops=2 * 27 * filters * depth * nv * planes * cells,
            bytes_accessed=2 * 27 * filters * depth, transcendentals=0),
    )(blocks, taps)
    summed = jnp.transpose(total, (1, 0, 2)) + bias[:, None, None]
    return summed.astype(jnp.bfloat16)


def solution(mesh):
    in_specs = (P("filt", "vox", None), P(None, "filt", "vox"), P("filt"))
    out_specs = P("filt", "vox", None)
    work = functools.partial(shards, mesh.shape["vox"], mesh.shape["filt"])
    return jax.shard_map(work, mesh=mesh, in_specs=in_specs, out_specs=out_specs, check_vma=False)
```

time: 43.7 us -> 42.3 us (0.968)
  the two profiles are of different devices: /device:TPU:28 before, /device:TPU:0 now
where the time goes in v2:
time: 42.3 us; the launch traced here: 42.1 us
  Pallas kernels  38.7 us (91%)
  local copies, waits for them, and re-layouts  2.34 us (6%)
  other arithmetic  1.04 us (2%)
    pallas_call x1, Pallas kernels, shards(): pl.pallas_call(functools.partial(body, nv, rep), out_shape=jax.ShapeDtype...  38.7 us
    unnamed x3, local copies, waits for them, and re-layouts  1.58 us
    convert_element_type x1, other arithmetic, shards(): return summed.astype(jnp.bfloat16)  1.04 us

profile of v2, /device:TPU:0, one launch (start us, length us, event | category | flops | bytes accessed | tf_op | source)
XLA Modules:
  0.0 42.1 jit_solution(1029486320639430104)
XLA Ops:
  0.0 1.6 %copy.7 = bf16[128,4,128]{2,0,1:T(8,128)(2,1)} copy(bf16[128,4,128]{2,1,0:T(4,128)(2,1)} %param.3) | data formatting | bytes 262144 | tf_op args[0]
  1.6 0.0 copy-start
  1.6 38.7 %shard_map.37 = f32[4,128,128]{2,1,0:T(8,128)} custom-call(bf16[4,128,128]{2,1,0:T(8,128)(2,1)} %bitcast.6, bf16[3,9,128,256]{3,2,1,0:T(8,128)(2,1)} %bitcast.7), custom_call_target="tpu_custom_call" | custom-call | flops 3623878656 | bytes 1769472 | tf_op jit(solution)/shard_map/pallas_call | solution.py:303
  40.3 0.0 copy-done
  40.3 1.0 %fusion = bf16[128,4,128]{2,0,1:T(8,128)(2,1)S(1)} fusion(f32[4,128,128]{2,1,0:T(8,128)} %shard_map.37, f32[128]{0:T(128)S(1)} %copy-done), kind=kLoop, calls=%fused_computation.1 | loop fusion | flops 131072 | bytes 393728 | tf_op jit(solution)/shard_map/convert_element_type | solution.py:327
  41.3 0.8 %copy.5 = bf16[128,4,128]{2,1,0:T(4,128)(2,1)} copy(bf16[128,4,128]{2,0,1:T(8,128)(2,1)S(1)} %fusion) | data formatting | bytes 262144 | tf_op jit(solution)/shard_map/convert_element_type | solution.py:327
Async XLA Ops:
  1.6 38.7 %copy-start = (f32[128]{0:T(128)S(1)}, f32[128]{0:T(128)}, u32[]{:S(2)}) copy-start(f32[128]{0:T(128)} %param.5) | copy-start | bytes 1540

commit v3 on v2

--- a/solution.py
+++ b/solution.py
@@ -318,7 +318,7 @@
             dma((rep, nv, CHUNKS)), dma((rep, nv, CHUNKS)), dma((half, steps)), dma((half, steps)), dma((half, steps)), dma((half, steps)),
         ],
         compiler_params=pltpu.CompilerParams(
-            collective_id=0, has_side_effects=True, vmem_limit_bytes=60 * 1024 * 1024),
+            collective_id=0, has_side_effects=True, vmem_limit_bytes=53 * 1024 * 1024),
         cost_estimate=pl.CostEstimate(
             flops=2 * 27 * filters * depth * nv * planes * cells,
             bytes_accessed=2 * 27 * filters * depth, transcendentals=0),

time: 42.3 us -> 39.1 us (0.924)
  Pallas kernels: 38.7 us -> 37.1 us
  other arithmetic: 1.04 us -> 0.09 us
  local copies, waits for them, and re-layouts: 2.34 us -> 1.69 us
    pallas_call x1, Pallas kernels: 38.7 us -> 37.1 us  [shards(): pl.pallas_call(functools.partial(body, nv, rep), out_shape=jax.ShapeDtype...]
    convert_element_type x1, other arithmetic: 1.04 us -> 0.09 us  [shards(): return summed.astype(jnp.bfloat16)]
    unnamed x3, local copies, waits for them, and re-layouts: 1.58 us -> 0.93 us
where the time goes in v3:
time: 39.1 us; the launch traced here: 38.9 us
  Pallas kernels  37.1 us (95%)
  local copies, waits for them, and re-layouts  1.69 us (4%)
    pallas_call x1, Pallas kernels, shards(): pl.pallas_call(functools.partial(body, nv, rep), out_shape=jax.ShapeDtype...  37.1 us
    unnamed x3, local copies, waits for them, and re-layouts  0.93 us

profile of v3, /device:TPU:0, one launch (start us, length us, event | category | flops | bytes accessed | tf_op | source)
XLA Modules:
  0.0 38.9 jit_solution(9902787700891811522)
XLA Ops:
  0.0 0.9 %copy.7 = bf16[128,4,128]{2,0,1:T(8,128)(2,1)S(1)} copy(bf16[128,4,128]{2,1,0:T(4,128)(2,1)} %param.3) | data formatting | bytes 262144 | tf_op args[0]
  0.9 0.0 copy-start
  0.9 37.1 %shard_map.37 = f32[4,128,128]{2,1,0:T(8,128)S(1)} custom-call(bf16[4,128,128]{2,1,0:T(8,128)(2,1)S(1)} %bitcast.6, bf16[3,9,128,256]{3,2,1,0:T(8,128)(2,1)} %bitcast.7), custom_call_target="tpu_custom_call" | custom-call | flops 3623878656 | bytes 1769472 | tf_op jit(solution)/shard_map/pallas_call | solution.py:303
  38.1 0.0 copy-done
  38.1 0.1 fusion
  38.2 0.8 %copy.5 = bf16[128,4,128]{2,1,0:T(4,128)(2,1)} copy(bf16[128,4,128]{2,0,1:T(8,128)(2,1)S(1)} %fusion) | data formatting | bytes 262144 | tf_op jit(solution)/shard_map/convert_element_type | solution.py:327
Async XLA Ops:
  0.9 37.1 %copy-start = (f32[128]{0:T(128)S(1)}, f32[128]{0:T(128)}, u32[]{:S(2)}) copy-start(f32[128]{0:T(128)} %param.5) | copy-start | bytes 1540
